TPU v7x, 512 devices: a whole 4x8x8 slice. The times are simulated.
512 devices in a mesh: grp: 16 (over x, y_lo, core), wide: 32 (over z, y_hi).
Axes of the slice: x: 4, y: 8 (y_hi: 4, y_lo: 2; y = y_hi * 2 + y_lo), z: 8, core: 2. Of those that a mesh axis runs over, the one named last changes fastest.
Arguments:
- queries: bfloat16 [2, 4, 128, 576], replicated
- cache: bfloat16 [2, 1048576, 576], P(None, ('grp', 'wide'))
- lengths: int32 [2], replicated, may hold values from 128 to 1048576, as said below
- up_weight: bfloat16 [128, 512, 128], P('grp'), may hold values from -0.25 to 0.25
- out_weight: bfloat16 [16384, 7168], P('grp', 'wide'), may hold values from -0.046875 to 0.046875
Outputs:
- mixed: float32 [2, 4, 7168], P(None, None, 'wide')
Inputs may be any that keep to these rules, and one draw needn't show every extreme that they name: `lengths`: multiples of 128; one sequence fills all 1048576 positions, the other is shorter.
All inputs are finite; a program needn't handle non-finite values.
Results may differ from a plain program's by a relative error of at most 0.00085.
Values sent between devices are 32-bit elements; how exact they have to be, the bound alone decides.
No kernel may reach another device: no remote copies, remote signals or barrier semaphores. Data moves between devices by JAX's collectives and lax.ppermute only.
A program may use at most 128 MiB of HBM per device.

v0:
```python
import math

import jax
import jax.numpy as jnp
from jax import lax
from jax.sharding import PartitionSpec as P

softmax_factor = 1.0 / math.sqrt(192.0) * (0.1 * math.log(40.0) + 1.0) ** 2
floor_value = -1e30


def combined_all(part, axis, combine):
    gathered = jax.tree.map(lambda a: lax.all_gather(a, axis), part)

    def take(source):
        return jax.tree.map(lambda a: lax.dynamic_index_in_dim(a, source, 0, False), gathered)

    return lax.fori_loop(
        1, lax.axis_size(axis), lambda source, state: combine(state, take(source)), take(0)
    )


def combine(first, second_part):
    acc_a, top_a, total_a = first
    acc_b, top_b, total_b = second_part
    peak = jnp.maximum(top_a, top_b)
    scale_a = jnp.exp(top_a - peak)
    scale_b = jnp.exp(top_b - peak)
    return (
        acc_a * scale_a[..., None] + acc_b * scale_b[..., None],
        peak,
        total_a * scale_a + total_b * scale_b,
    )


def fold_sources(parts):
    acc, tops, totals = parts
    peak = jnp.max(tops, axis=0)
    scales = jnp.exp(tops - peak[None])
    return (jnp.sum(acc * scales[..., None], axis=0), peak, jnp.sum(totals * scales, axis=0))


def body(queries, cache, lengths, up_weight, out_weight):
    rows, draft, heads, key_dim = queries.shape
    span = cache.shape[1]
    latent = up_weight.shape[1]
    owned = up_weight.shape[0]
    start = (lax.axis_index("grp") * lax.axis_size("wide") + lax.axis_index("wide")) * span
    positions = start + jnp.arange(span, dtype=jnp.int32)
    query_pos = jnp.arange(draft * heads, dtype=jnp.int32) // heads
    acc_list = []
    top_list = []
    total_list = []
    for row in range(rows):
        flattened = queries[row].reshape(draft * heads, key_dim)
        cache_block = cache[row]
        logit_scores = (
            lax.dot_general(
                flattened, cache_block, (((1,), (1,)), ((), ())), preferred_element_type=jnp.float32
            )
            * softmax_factor
        )
        limit = lengths[row] - draft + 1 + query_pos
        visible = positions[None, :] < limit[:, None]
        local = jnp.max(jnp.where(visible, logit_scores, floor_value), axis=-1)
        weights = jnp.where(visible, jnp.exp(logit_scores - local[:, None]), 0.0).astype(
            jnp.bfloat16
        )
        total_list.append(jnp.sum(weights.astype(jnp.float32), axis=-1))
        top_list.append(local)
        acc_list.append(
            jnp.dot(weights, cache_block[:, :latent], preferred_element_type=jnp.float32)
        )
    acc = jnp.stack(acc_list).reshape(1, rows * draft, heads, latent)
    tops = jnp.stack(top_list).reshape(1, rows * draft, heads)
    totals = jnp.stack(total_list).reshape(1, rows * draft, heads)
    parts = (
        lax.all_to_all(acc, "grp", split_axis=2, concat_axis=0, tiled=True),
        lax.all_to_all(tops, "grp", split_axis=2, concat_axis=0, tiled=True),
        lax.all_to_all(totals, "grp", split_axis=2, concat_axis=0, tiled=True),
    )
    own_acc, own_top, own_total = fold_sources(parts)
    up_wide = up_weight.astype(jnp.float32)
    own_acc, own_top, own_total = combined_all((own_acc, own_top, own_total), "wide", combine)
    values = jnp.einsum(
        "rhc,hcv->rhv", own_acc / own_total[..., None], up_wide, precision=lax.Precision.HIGHEST
    )
    partial_out = jnp.dot(
        values.reshape(rows * draft, owned * values.shape[2]),
        out_weight.astype(jnp.float32),
        precision=lax.Precision.HIGHEST,
    )
    mixed = lax.psum(partial_out, "grp")
    return mixed.reshape(rows, draft, out_weight.shape[1])


def solution(mesh):
    in_specs = (P(), P(None, ("grp", "wide"), None), P(), P("grp", None, None), P("grp", "wide"))
    out_specs = P(None, None, "wide")
    return jax.shard_map(body, mesh=mesh, in_specs=in_specs, out_specs=out_specs, check_vma=False)
```

profile of v0, /device:TPU:1, one launch (start us, length us, event | category | flops | bytes accessed | tf_op | source)
XLA Modules:
  0.0 318.9 jit_solution(11678780335582461850)
XLA Ops:
  6.5 1.4 fusion.36
  9.3 1.5 fusion.35
  11.9 1.8 fusion.17
  13.8 2.8 fusion.3
  16.6 3.2 %convert_reduce_fusion.1 = (f32[512]{0:T(512)S(1)}, bf16[512,2048]{1,0:T(8,128)(2,1)}, f32[512]{0:T(512)S(1)}, bf16[512,2048]{1,0:T(8,128)(2,1)S(1)}) fusion(f32[512]{0:T(512)S(1)} %get-tuple-element.184, f32[512,2048]{1,0:T(8,128)S(1)} %get-tuple-element.218, s32[512]{0:T(512)S(1)} %get-tuple-element.220, s32[2048]{0:T(1024)S(1)} %iota_add_fusion, ...), kind=kLoop, calls=%fused_computation.17 | loop fusion | flops 14679040 | bytes 12603392 | tf_op jit(solution)/shard_map/reduce_sum | solution.py:69
  20.6 10.2 %all-to-all-start.2 = ((f32[1,8,128]{1,0,2:T(1,128)}), f32[1,8,128]{1,0,2:T(1,128)S(1)}, u32[]{:S(2)}, u32[]{:S(2)}) async-start(f32[1,8,128]{1,0,2:T(1,128)} %copy.33), calls=%async_computation.2 | async-start | bytes 131072 | tf_op jit(solution)/shard_map/all_to_all | solution.py:80
  30.8 2.9 slice_bitcast_fusion.1
  33.8 2.3 fusion.11
  36.1 2.3 fusion.14
  39.1 5.8 %all-to-all-start.1 = ((f32[1,8,128]{1,0,2:T(1,128)}), f32[1,8,128]{1,0,2:T(1,128)S(1)}, u32[]{:S(2)}, u32[]{:S(2)}) async-start(f32[1,8,128]{1,0,2:T(1,128)} %copy.29), calls=%async_computation.1 | async-start | bytes 131072 | tf_op jit(solution)/shard_map/all_to_all | solution.py:79
  44.9 1.7 pad_maximum_fusion
  46.6 2.6 copy.28
  49.2 1.5 all-to-all-done.1
  50.7 4.2 %all-to-all-start = ((f32[1,8,128,512]{3,1,0,2:T(8,128)}), f32[1,8,128,512]{3,1,0,2:T(8,128)S(1)}, u32[]{:S(2)}, u32[]{:S(2)}) async-start(f32[1,8,128,512]{3,1,0,2:T(8,128)} %copy.28), calls=%async_computation | async-start | bytes 4194304 | tf_op jit(solution)/shard_map/all_to_all | solution.py:78
  55.3 26.7 %all-to-all-done = f32[1,8,128,512]{3,1,0,2:T(8,128)S(1)} async-done(((f32[1,8,128,512]{3,1,0,2:T(8,128)}), f32[1,8,128,512]{3,1,0,2:T(8,128)S(1)}, u32[]{:S(2)}, u32[]{:S(2)}) %all-to-all-start) | async-done | bytes 2097184 | tf_op jit(solution)/shard_map/all_to_all | solution.py:78
  83.0 72.4 %all-gather.2 = f32[256,8]{1,0:T(8,128)S(1)} all-gather(f32[8,8]{1,0:T(8,128)S(1)} %get-tuple-element.204), channel_id=4, replica_groups=mesh['grp'=16,'wide'=32] {'wide'}, dimensions={0}, use_global_device_ids=true | all-gather | bytes 8448 | tf_op jit(solution)/shard_map/all_gather | solution.py:13
  155.4 68.4 %all-gather.1 = f32[256,8]{1,0:T(8,128)S(1)} all-gather(f32[8,8]{1,0:T(8,128)S(1)} %bitcast_reduce_fusion), channel_id=3, replica_groups=mesh['grp'=16,'wide'=32] {'wide'}, dimensions={0}, use_global_device_ids=true | all-gather | bytes 8448 | tf_op jit(solution)/shard_map/all_gather | solution.py:13
  224.8 32.5 %while.19 = (s32[]{:T(128)}, f32[8,8,512]{2,1,0:T(8,128)S(1)}, f32[8,8]{1,0:T(8,128)S(1)}, f32[8,8]{1,0:T(8,128)S(1)}, f32[32,8,8]{2,1,0:T(8,128)S(1)}, /*index=...) while((s32[]{:T(128)}, f32[8,8,512]{2,1,0:T(8,128)S(1)}, ...), condition=%wide.region_8.9_spmd, body=%wide.region_7.8_spmd.sunk | while | flops 98693 | bytes 395927 | solution.py:18
  224.8 1.0 fusion.46
  225.9 1.0 fusion.46
  226.9 1.0 fusion.46
  228.0 1.0 fusion.46
  229.0 1.0 fusion.46
  230.1 1.0 fusion.46
  231.1 1.0 fusion.46
  232.2 1.0 fusion.46
  233.2 1.0 fusion.46
  234.3 1.0 fusion.46
  235.3 1.0 fusion.46
  236.4 1.0 fusion.46
  237.4 1.0 fusion.46
  258.5 53.6 %psum.7 = f32[2,4,224]{2,1,0:T(4,128)} all-reduce(f32[2,4,224]{2,1,0:T(4,128)S(1)} %reshape.56), channel_id=1, replica_groups=mesh['grp'=16,'wide'=32] {'grp'}, use_global_device_ids=true, to_apply=%region_9.10 | all-reduce | flops 1792 | bytes 14336 | tf_op jit(solution)/shard_map/psum | solution.py:93
  (85 shorter events, 24.7 us)
Async XLA Ops:
  6.5 250.9 %copy-start = (bf16[8,512,128]{2,1,0:T(8,128)(2,1)S(1)}, bf16[8,512,128]{2,1,0:T(8,128)(2,1)}, u32[]{:S(2)}) copy-start(bf16[8,512,128]{2,1,0:T(8,128)(2,1)} %param.10) | copy-start | bytes 3145732
  9.2 2.7 copy-start.1
  20.6 18.5 %all-to-all-start.2 = ((f32[1,8,128]{1,0,2:T(1,128)}), f32[1,8,128]{1,0,2:T(1,128)S(1)}, u32[]{:S(2)}, u32[]{:S(2)}) async-start(f32[1,8,128]{1,0,2:T(1,128)} %copy.33), calls=%async_computation.2 | async-start | bytes 131072 | tf_op jit(solution)/shard_map/all_to_all | solution.py:80
  30.8 3.0 copy-start.2
  39.1 11.6 %all-to-all-start.1 = ((f32[1,8,128]{1,0,2:T(1,128)}), f32[1,8,128]{1,0,2:T(1,128)S(1)}, u32[]{:S(2)}, u32[]{:S(2)}) async-start(f32[1,8,128]{1,0,2:T(1,128)} %copy.29), calls=%async_computation.1 | async-start | bytes 131072 | tf_op jit(solution)/shard_map/all_to_all | solution.py:79
  50.7 31.3 %all-to-all-start = ((f32[1,8,128,512]{3,1,0,2:T(8,128)}), f32[1,8,128,512]{3,1,0,2:T(8,128)S(1)}, u32[]{:S(2)}, u32[]{:S(2)}) async-start(f32[1,8,128,512]{3,1,0,2:T(8,128)} %copy.28), calls=%async_computation | async-start | bytes 4194304 | tf_op jit(solution)/shard_map/all_to_all | solution.py:78
  54.9 168.9 %all-gather.5.cloned.1.call-start = ((), (), s32[]{:S(2)}) async-start(), calls=%async_computation.3 | async-start | bytes 4325376 | tf_op jit(solution)/shard_map/all_gather | solution.py:13
  82.2 175.8 %copy-start.3 = (bf16[1024,224]{0,1:T(8,128)(2,1)S(1)}, bf16[1024,224]{0,1:T(8,128)(2,1)}, u32[]{:S(2)}) copy-start(bf16[1024,224]{0,1:T(8,128)(2,1)} %param.11) | copy-start | bytes 1376260
Sparse Core Ops, SparseCore 0:
  83.1 100.9 all-gather.4
where the time goes:
time: 320 us; the launch traced here: 319 us
  blocking collectives  194 us (61%)
  other arithmetic  36.8 us (11%)
  waiting for transfers between devices  28.3 us (9%)
  starting transfers between devices  20.2 us (6%)
  between operations  14.9 us (5%)
  local copies, waits for them, and re-layouts  13 us (4%)
  matrix products  10.3 us (3%)
    all_gather x2, blocking collectives, combined_all(): gathered = jax.tree.map(lambda a: lax.all_gather(a, axis), part)  141 us
    psum x1, blocking collectives, body(): mixed = lax.psum(partial_out, 'grp')  53.6 us
    add x31, other arithmetic, combine(): acc_a * scale_a[..., None] + acc_b * scale_b[..., None]  31 us
    all_to_all x1, waiting for transfers between devices, body(): lax.all_to_all(acc, 'grp', split_axis=2, concat_axis=0, tiled=True)  26.7 us
    all_to_all x1, starting transfers between devices, body(): lax.all_to_all(totals, 'grp', split_axis=2, concat_axis=0, tiled=True)  10.2 us
  transfers between devices with their start and end apart: 4, of which 2 were waited for; matrix products, arithmetic and copies ran while one was open for 4% of the time, Pallas kernels for 0%

commit v1 on v0

v1 whole, which is shorter than its diff:
```python
import math

import jax
import jax.numpy as jnp
from jax import lax
from jax.experimental import pallas as pl
from jax.experimental.pallas import tpu as pltpu
from jax.sharding import PartitionSpec as P

softmax_factor = 1.0 / math.sqrt(192.0) * (0.1 * math.log(40.0) + 1.0) ** 2
score_scale = softmax_factor * math.log2(math.e)
floor_value = -1e30
floor_guard = -5e29

LANES = 128
SUB = 8


def split_dot(x, w, contract=0):
    rows = x.shape[0]
    high = x.astype(jnp.bfloat16)
    low = (x - high.astype(jnp.float32)).astype(jnp.bfloat16)
    both = lax.dot_general(jnp.concatenate([high, low], axis=0), w, (((1,), (contract,)), ((), ())),
                           preferred_element_type=jnp.float32)
    return both[:rows] + both[rows:]


def attend(queries, cache, lengths, groups, latent):
    rows, draft, key_dim, heads = queries.shape
    span = cache.shape[2]
    owned = heads // groups
    pairs = groups // 2
    lat_tiles = latent // LANES
    count = rows * draft
    tiles = count * lat_tiles + 1
    qrows = draft * heads

    def kernel(q_hbm, cache_hbm, len_ref, keep_hbm, send_hbm,
               q_v, k_v, s_v, acc_v, top_v, tot_v, stat_v, q_sem, k_sem, out_sem):
        grp = lax.axis_index("grp")
        core = lax.rem(grp, 2)
        start = (grp * lax.axis_size("wide") + lax.axis_index("wide")) * span
        q_copies = [pltpu.make_async_copy(q_hbm.at[b], q_v.at[b], q_sem.at[b]) for b in range(rows)]
        k_copies = [pltpu.make_async_copy(cache_hbm.at[b], k_v.at[b], k_sem.at[b]) for b in range(rows)]
        for b in range(rows):
            q_copies[b].start()
            k_copies[b].start()
        out_copies = []

        def send_out(view, tile_at, n_tiles, slot):
            for i, (dst, flip) in enumerate(((send_hbm, 1), (keep_hbm, 0))):
                copy = pltpu.make_async_copy(
                    view(jnp.bitwise_xor(core, flip)), dst.at[:, pl.ds(tile_at, n_tiles)], out_sem.at[i, slot])
                copy.start()
                out_copies.append(copy)

        pos = start + lax.broadcasted_iota(jnp.int32, (1, span), 1)
        for b in range(rows):
            q_copies[b].wait()
            k_copies[b].wait()
            tops = []
            for j in range(draft):
                s = lax.dot_general(q_v[b, j], k_v[b], (((0,), (0,)), ((), ())),
                                    preferred_element_type=jnp.float32) * score_scale
                s = jnp.where(pos < len_ref[b] - draft + 1 + j, s, floor_value)
                s_v[b, j * heads:(j + 1) * heads, :] = s
                running = s[:, :LANES]
                for c in range(1, span // LANES):
                    running = jnp.maximum(running, s[:, c * LANES:(c + 1) * LANES])
                tops.append(running)
            top = jnp.max(jnp.concatenate(tops, axis=0), axis=-1, keepdims=True)
            top_v[b] = jnp.broadcast_to(top, (qrows, LANES))
            w = jnp.exp2(s_v[b] - jnp.maximum(top, floor_guard)).astype(jnp.bfloat16)
            wide_w = w.astype(jnp.float32)
            total = wide_w[:, :LANES]
            for c in range(1, span // LANES):
                total = total + wide_w[:, c * LANES:(c + 1) * LANES]
            acc = lax.dot_general(w, k_v[b, :latent, :], (((1,), (1,)), ((), ())),
                                  preferred_element_type=jnp.float32)
            tot_v[b] = jnp.broadcast_to(jnp.sum(total, axis=-1, keepdims=True), (qrows, LANES))
            for j in range(draft):
                block = acc[j * heads:(j + 1) * heads].reshape(pairs, 2, owned, latent)
                for c in range(lat_tiles):
                    acc_v[b, j, :, :, c] = block[:, :, :, c * LANES:(c + 1) * LANES]
            for j in range(draft):
                r = b * draft + j
                send_out(lambda bit: acc_v.at[b, j, :, bit], r * lat_tiles, lat_tiles, r)
        lane = lax.broadcasted_iota(jnp.int32, (owned, LANES), 1)
        for g in range(groups):
            stat = jnp.zeros((owned, LANES), jnp.float32)
            for r in range(count):
                b, j = r // draft, r % draft
                at = slice(j * heads + g * owned, j * heads + (g + 1) * owned)
                stat = jnp.where(lane == r, top_v[b, at, :], stat)
                stat = jnp.where(lane == count + r, tot_v[b, at, :], stat)
            stat_v[g // 2, g % 2, 0] = stat
        send_out(lambda bit: stat_v.at[:, bit], tiles - 1, 1, count)
        for copy in out_copies:
            copy.wait()

    message = jax.ShapeDtypeStruct((pairs, tiles, owned, LANES), jnp.float32)
    any_space = pl.BlockSpec(memory_space=pl.ANY)
    return pl.pallas_call(
        kernel,
        out_shape=(message, message),
        in_specs=[any_space, any_space, pl.BlockSpec(memory_space=pltpu.SMEM)],
        out_specs=(any_space, any_space),
        scratch_shapes=[
            pltpu.VMEM((rows, draft, key_dim, heads), jnp.bfloat16),
            pltpu.VMEM((rows, key_dim, span), jnp.bfloat16),
            pltpu.VMEM((rows, qrows, span), jnp.float32),
            pltpu.VMEM((rows, draft, pairs, 2, lat_tiles, owned, LANES), jnp.float32),
            pltpu.VMEM((rows, qrows, LANES), jnp.float32),
            pltpu.VMEM((rows, qrows, LANES), jnp.float32),
            pltpu.VMEM((pairs, 2, 1, owned, LANES), jnp.float32),
            pltpu.SemaphoreType.DMA((rows,)),
            pltpu.SemaphoreType.DMA((rows,)),
            pltpu.SemaphoreType.DMA((2, count + 1)),
        ],
        compiler_params=pltpu.CompilerParams(vmem_limit_bytes=63 << 20),
        name="attend",
    )(queries, cache, lengths)


def fold_stats(stats, count):
    peak = stats[0]
    for s in stats[1:]:
        peak = jnp.maximum(peak, s)
    scales = [jnp.exp2(s - peak) for s in stats]
    total = None
    for s, e in zip(stats, scales):
        part = pltpu.roll(s, LANES - count, 1) * e
        total = part if total is None else total + part
    lane = lax.broadcasted_iota(jnp.int32, peak.shape, 1)
    joint = jnp.where(lane < count, peak, pltpu.roll(total, count, 1))
    return scales, total, jnp.where(lane < 2 * count, joint, 0.0)


def add_cores(keep, other, count):
    pairs, tiles = keep.shape[:2]
    per = (tiles - 1) // count

    def kernel(a_ref, b_ref, o_ref):
        for a in range(a_ref.shape[0]):
            scales, _, joint = fold_stats([a_ref[a, tiles - 1], b_ref[a, tiles - 1]], count)
            o_ref[a, tiles - 1] = joint
            for r in range(count):
                ea = scales[0][:, r:r + 1]
                eb = scales[1][:, r:r + 1]
                for c in range(per):
                    t = r * per + c
                    o_ref[a, t] = a_ref[a, t] * ea + b_ref[a, t] * eb

    steps = 4
    spec = pl.BlockSpec((pairs // steps,) + keep.shape[1:], lambda i: (i, 0, 0, 0))
    return pl.pallas_call(
        kernel,
        grid=(steps,),
        out_shape=jax.ShapeDtypeStruct(keep.shape, jnp.float32),
        in_specs=[spec, spec],
        out_specs=spec,
        compiler_params=pltpu.CompilerParams(vmem_limit_bytes=32 << 20),
        name="add_cores",
    )(keep, other)


def up_project(parts, up_weight, count, copies):
    sources, tiles = parts.shape[:2]
    owned, latent, value_dim = up_weight.shape
    per = (tiles - 1) // count

    def kernel(p_ref, u_ref, o_ref, lat_v):
        scales, _, joint = fold_stats([p_ref[s, tiles - 1] for s in range(sources)], count)
        for r in range(count):
            es = [jnp.broadcast_to(e[:, r:r + 1], (SUB, LANES)) for e in scales]
            for c in range(per):
                t = r * per + c
                total = p_ref[0, t] * es[0]
                for s in range(1, sources):
                    total = total + p_ref[s, t] * es[s]
                lat_v[c, r * SUB:(r + 1) * SUB, :] = total
        row = lax.broadcasted_iota(jnp.int32, (count * SUB, value_dim), 0) % SUB
        lat = jnp.concatenate([lat_v[c] for c in range(per)], axis=1)
        values = jnp.zeros((count * SUB, value_dim), jnp.float32)
        for h in range(owned):
            values = jnp.where(row == h, split_dot(lat, u_ref[h]), values)
        for i in range(copies):
            for r in range(count):
                o_ref[i, r] = values[r * SUB:(r + 1) * SUB]
            o_ref[i, count] = joint

    return pl.pallas_call(
        kernel,
        out_shape=jax.ShapeDtypeStruct((copies, count + 1, SUB, LANES), jnp.float32),
        scratch_shapes=[pltpu.VMEM((per, count * SUB, LANES), jnp.float32)],
        compiler_params=pltpu.CompilerParams(vmem_limit_bytes=32 << 20),
        name="up_project",
    )(parts, up_weight)


def add_wide(parts, count, copies):
    sources = parts.shape[0]

    def kernel(p_ref, o_ref):
        scales, _, joint = fold_stats([p_ref[s, count] for s in range(sources)], count)
        for r in range(count):
            value = None
            for s in range(sources):
                part = p_ref[s, r] * scales[s][:, r:r + 1]
                value = part if value is None else value + part
            for i in range(copies):
                o_ref[i, r] = value
        for i in range(copies):
            o_ref[i, count] = joint

    return pl.pallas_call(
        kernel,
        out_shape=jax.ShapeDtypeStruct((copies,) + parts.shape[1:], jnp.float32),
        compiler_params=pltpu.CompilerParams(vmem_limit_bytes=32 << 20),
        name="add_wide",
    )(parts)


def out_project(parts, out_weight, count, copies):
    sources = parts.shape[0]
    features = out_weight.shape[0]

    def kernel(p_ref, w_ref, o_ref, val_v):
        scales, total, _ = fold_stats([p_ref[s, count] for s in range(sources)], count)
        inverse = 1.0 / total
        for r in range(count):
            value = None
            for s in range(sources):
                part = p_ref[s, r] * scales[s][:, r:r + 1]
                value = part if value is None else value + part
            val_v[r * SUB:(r + 1) * SUB, :] = value * inverse[:, r:r + 1]
        values = jnp.concatenate([val_v[pl.ds(h, count, stride=SUB), :] for h in range(SUB)], axis=1)
        mixed = split_dot(values, w_ref[...], 1)
        for i in range(copies):
            o_ref[i] = mixed

    return pl.pallas_call(
        kernel,
        out_shape=jax.ShapeDtypeStruct((copies, count, features), jnp.float32),
        scratch_shapes=[pltpu.VMEM((count * SUB, LANES), jnp.float32)],
        compiler_params=pltpu.CompilerParams(vmem_limit_bytes=32 << 20),
        name="out_project",
    )(parts, out_weight)


def body(queries, cache, lengths, up_weight, out_weight):
    rows, draft = queries.shape[:2]
    count = rows * draft
    groups = lax.axis_size("grp")
    wide = lax.axis_size("wide")
    near = 4
    same_core = [list(range(c, groups, 2)) for c in range(2)]
    along_y = [list(range(z, z + near)) for z in range(0, wide, near)]
    along_z = [list(range(y, wide, near)) for y in range(near)]
    keep, send = attend(jnp.swapaxes(queries, 2, 3), jnp.swapaxes(cache, 1, 2), lengths, groups, up_weight.shape[1])
    other = lax.ppermute(send, "grp", [(i, i ^ 1) for i in range(groups)])
    mine = add_cores(keep, other, count)
    parts = lax.all_to_all(mine, "grp", 0, 0, axis_index_groups=same_core, tiled=True)
    values = up_project(parts, up_weight, count, near)
    values = lax.all_to_all(values, "wide", 0, 0, axis_index_groups=along_y, tiled=True)
    values = add_wide(values, count, wide // near)
    values = lax.all_to_all(values, "wide", 0, 0, axis_index_groups=along_z, tiled=True)
    mixed = out_project(values, out_weight.T, count, groups)
    mixed = lax.all_to_all(mixed, "grp", 0, 0, tiled=True)
    return jnp.sum(mixed, axis=0).reshape(rows, draft, mixed.shape[2])


def solution(mesh):
    in_specs = (P(), P(None, ("grp", "wide"), None), P(), P("grp", None, None), P("grp", "wide"))
    out_specs = P(None, None, "wide")
    return jax.shard_map(body, mesh=mesh, in_specs=in_specs, out_specs=out_specs, check_vma=False)
```

time: 320 us -> 87 us (0.27)
  blocking collectives: 194 us -> 61.4 us
  other arithmetic: 36.8 us -> 0.02 us
  waiting for transfers between devices: 28.3 us -> 2.52 us
  between operations: 14.9 us -> 0.06 us
  Pallas kernels: 0 us -> 12.1 us
  starting transfers between devices: 20.2 us -> 8.78 us
  local copies, waits for them, and re-layouts: 13 us -> 1.86 us
  matrix products: 10.3 us -> 0 us
    all_gather x2 -> x0, blocking collectives: 141 us -> none  [combined_all(): gathered = jax.tree.map(lambda a: lax.all_gather(a, axis), part)]
    all_to_all x0 -> x4, blocking collectives: none -> 61.4 us  [the longest x1 19.5 us: body(): lax.all_to_all(values, 'wide', 0, 0, axis_index_groups=along_z, tiled=True)]
    psum x1 -> x0, blocking collectives: 53.6 us -> none  [body(): mixed = lax.psum(partial_out, 'grp')]
    add x64 -> x0, other arithmetic: 31.5 us -> none  [the longest x31 31 us: combine(): acc_a * scale_a[..., None] + acc_b * scale_b[..., None]]
    all_to_all x3 -> x0, waiting for transfers between devices: 28.3 us -> none  [the longest x1 26.7 us: body(): lax.all_to_all(acc, 'grp', split_axis=2, concat_axis=0, tiled=True)]
    all_to_all x3 -> x0, starting transfers between devices: 20.1 us -> none  [the longest x1 10.2 us: body(): lax.all_to_all(totals, 'grp', split_axis=2, concat_axis=0, tiled=True)]
    pallas_call x0 -> x5, Pallas kernels: none -> 12.1 us  [the longest x1 10.4 us: attend(): pl.pallas_call(kernel, out_shape=(message, message), in_specs=[any_space,...]
    dot_general x6 -> x0, matrix products: 10.3 us -> none  [the longest x2 4.67 us: body(): lax.dot_general(flattened, cache_block, (((1,), (1,)), ((), ())), preferr...]
  transfers between devices with their start and end apart: 4 -> 1, of which waited for: 2 -> 1; matrix products, arithmetic and copies ran while one was open for 4% -> 0% of each run, Pallas kernels for 0% -> 0%
where the time goes in v1:
time: 87 us; the launch traced here: 86.7 us
  blocking collectives  61.4 us (71%)
  Pallas kernels  12.1 us (14%)
  starting transfers between devices  8.78 us (10%)
  waiting for transfers between devices  2.52 us (3%)
  local copies, waits for them, and re-layouts  1.86 us (2%)
    all_to_all x1, blocking collectives, body(): lax.all_to_all(values, 'wide', 0, 0, axis_index_groups=along_z, tiled=True)  19.5 us
    all_to_all x1, blocking collectives, body(): lax.all_to_all(mine, 'grp', 0, 0, axis_index_groups=same_core, tiled=True)  18.4 us
    all_to_all x1, blocking collectives, body(): mixed = lax.all_to_all(mixed, 'grp', 0, 0, tiled=True)  13.5 us
    pallas_call x1, Pallas kernels, attend(): pl.pallas_call(kernel, out_shape=(message, message), in_specs=[any_space,...  10.4 us
    all_to_all x1, blocking collectives, body(): lax.all_to_all(values, 'wide', 0, 0, axis_index_groups=along_y, tiled=True)  9.92 us
    ppermute x1, starting transfers between devices, body(): other = lax.ppermute(send, 'grp', [(i, i ^ 1) for i in range(groups)])  8.78 us
    ppermute x1, waiting for transfers between devices, body(): other = lax.ppermute(send, 'grp', [(i, i ^ 1) for i in range(groups)])  2.52 us
  transfers between devices with their start and end apart: 1, of which 1 were waited for; matrix products, arithmetic and copies ran while one was open for 0% of the time, Pallas kernels for 0%

profile of v1, /device:TPU:1, one launch (start us, length us, event | category | flops | bytes accessed | tf_op | source)
XLA Modules:
  0.0 86.7 jit_solution(7947434426998591607)
XLA Ops:
  0.0 10.4 %attend.1 = (f32[8,33,8,128]{3,2,1,0:T(8,128)}, f32[8,33,8,128]{3,2,1,0:T(8,128)}) custom-call(bf16[2,4,576,128]{3,2,1,0:T(8,128)(2,1)} %bitcast.5, bf16[2,576,2048]{2,1,0:T(8,128)(2,1)} %bitcast.4, s32[2]{0:T(128)} %len_ref.1), custom_call_target="tpu_custom_call" | custom-call | tf_op jit(solution)/shard_map/attend/pallas_call | solution.py:103
  10.4 8.8 %collective-permute-start = (f32[8,33,8,128]{3,2,1,0:T(8,128)}, f32[8,33,8,128]{3,2,1,0:T(8,128)S(1)}, u32[]{:S(2)}, u32[]{:S(2)}) collective-permute-start(f32[8,33,8,128]{3,2,1,0:T(8,128)} %get-tuple-element.8), channel_id=1, source_target_pairs={{0,32},{32,0},{64,96},{96,64},{128,160},{160,128},{192,224},{224,1... | collective-permute-start | bytes 3244040 | tf_op jit(solution)/shard_map/ppermute | solution.py:261
  19.2 2.5 %collective-permute-done.b_ref = f32[8,33,8,128]{3,2,1,0:T(8,128)S(1)} collective-permute-done((f32[8,33,8,128]{3,2,1,0:T(8,128)}, f32[8,33,8,128]{3,2,1,0:T(8,128)S(1)}, u32[]{:S(2)}, u32[]{:S(2)}) %collective-permute-start) | collective-permute-done | bytes 1081376 | tf_op jit(solution)/shard_map/ppermute | solution.py:261
  21.7 0.0 copy-start
  21.7 1.2 %copy-done = f32[8,33,8,128]{3,2,1,0:T(8,128)S(1)} copy-done((f32[8,33,8,128]{3,2,1,0:T(8,128)S(1)}, f32[8,33,8,128]{3,2,1,0:T(8,128)}, u32[]{:S(2)}) %copy-start) | copy-done | bytes 1081368
  23.0 0.6 add_cores.1
  23.5 0.0 copy-start.1
  23.6 18.4 %all_to_all.20.p_ref = f32[8,33,8,128]{3,2,1,0:T(8,128)S(1)} all-to-all(f32[8,33,8,128]{3,2,1,0:T(8,128)S(1)} %add_cores.1), channel_id=1, replica_groups={{0,64,128,192,256,320,384,448},{32,96,160,224,288,352,416,480},{1,65,12..., dimensions={0} | all-to-all | bytes 2162688 | tf_op jit(solution)/shard_map/all_to_all | solution.py:263
  42.0 0.0 copy-done.1
  42.0 0.6 up_project.1
  42.6 0.0 copy-start.2
  42.6 9.9 %all_to_all.21.p_ref = f32[4,9,8,128]{3,2,1,0:T(8,128)S(1)} all-to-all(f32[4,9,8,128]{3,2,1,0:T(8,128)S(1)} %up_project.1), channel_id=1, replica_groups={{0,1,2,3},{4,5,6,7},{8,9,10,11},{12,13,14,15},{16,17,18,19},{20,21,22,2..., dimensions={0} | all-to-all | bytes 294912 | tf_op jit(solution)/shard_map/all_to_all | solution.py:265
  52.5 0.1 add_wide.1
  52.6 19.5 %all_to_all.22.p_ref = f32[8,9,8,128]{3,2,1,0:T(8,128)S(1)} all-to-all(f32[8,9,8,128]{3,2,1,0:T(8,128)S(1)} %add_wide.1), channel_id=1, replica_groups={{0,4,8,12,16,20,24,28},{1,5,9,13,17,21,25,29},{2,6,10,14,18,22,26,30},{..., dimensions={0} | all-to-all | bytes 589824 | tf_op jit(solution)/shard_map/all_to_all | solution.py:267
  72.2 0.0 copy-done.2
  72.2 0.4 out_project.1
  72.6 13.5 %all_to_all.23 = f32[16,8,224]{2,1,0:T(8,128)S(1)} all-to-all(f32[16,8,224]{2,1,0:T(8,128)S(1)} %out_project.1), channel_id=1, replica_groups=mesh['grp'=16,'wide'=32] {'grp'}, dimensions={0} | all-to-all | bytes 229376 | tf_op jit(solution)/shard_map/all_to_all | solution.py:269
  86.1 0.6 reshape.3
  (1 shorter events, 0.0 us)
Async XLA Ops:
  10.4 11.3 %collective-permute-start = (f32[8,33,8,128]{3,2,1,0:T(8,128)}, f32[8,33,8,128]{3,2,1,0:T(8,128)S(1)}, u32[]{:S(2)}, u32[]{:S(2)}) collective-permute-start(f32[8,33,8,128]{3,2,1,0:T(8,128)} %get-tuple-element.8), channel_id=1, source_target_pairs={{0,32},{32,0},{64,96},{96,64},{128,160},{160,128},{192,224},{224,1... | collective-permute-start | bytes 3244040 | tf_op jit(solution)/shard_map/ppermute | solution.py:261
  21.7 1.2 %copy-start = (f32[8,33,8,128]{3,2,1,0:T(8,128)S(1)}, f32[8,33,8,128]{3,2,1,0:T(8,128)}, u32[]{:S(2)}) copy-start(f32[8,33,8,128]{3,2,1,0:T(8,128)} %get-tuple-element.7.a_ref) | copy-start | bytes 3244036
  23.5 18.5 %copy-start.1 = (bf16[8,512,128]{2,1,0:T(8,128)(2,1)S(1)}, bf16[8,512,128]{2,1,0:T(8,128)(2,1)}, u32[]{:S(2)}) copy-start(bf16[8,512,128]{2,1,0:T(8,128)(2,1)} %u_ref.1) | copy-start | bytes 3145732
  42.6 29.6 %copy-start.2 = (bf16[1024,224]{0,1:T(8,128)(2,1)S(1)}, bf16[1024,224]{0,1:T(8,128)(2,1)}, u32[]{:S(2)}) copy-start(bf16[1024,224]{0,1:T(8,128)(2,1)} %param.9) | copy-start | bytes 1376260

commit v2 on v1

--- a/solution.py
+++ b/solution.py
@@ -14,6 +14,7 @@
 
 LANES = 128
 SUB = 8
+FIRST_PARTS = 2
 
 
 def split_dot(x, w, contract=0):
@@ -35,39 +36,37 @@
     tiles = count * lat_tiles + 1
     qrows = draft * heads
 
-    def kernel(q_hbm, cache_hbm, len_ref, keep_hbm, send_hbm,
-               q_v, k_v, s_v, acc_v, top_v, tot_v, stat_v, q_sem, k_sem, out_sem):
+    def pieces(b):
+        part = span // FIRST_PARTS if b == 0 else span
+        return [(lo, lo + part) for lo in range(0, span, part)]
+
+    def kernel(q_hbm, cache_hbm, len_ref, keep_ref, send_ref,
+               q_v, k_v, s_v, acc_v, top_v, tot_v, stat_v, q_sem, k_sem):
         grp = lax.axis_index("grp")
         core = lax.rem(grp, 2)
         start = (grp * lax.axis_size("wide") + lax.axis_index("wide")) * span
         q_copies = [pltpu.make_async_copy(q_hbm.at[b], q_v.at[b], q_sem.at[b]) for b in range(rows)]
-        k_copies = [pltpu.make_async_copy(cache_hbm.at[b], k_v.at[b], k_sem.at[b]) for b in range(rows)]
+        k_copies = [
+            [pltpu.make_async_copy(cache_hbm.at[b, :, pl.ds(lo, hi - lo)], k_v.at[b, :, pl.ds(lo, hi - lo)], k_sem.at[b, p])
+             for p, (lo, hi) in enumerate(pieces(b))] for b in range(rows)]
         for b in range(rows):
             q_copies[b].start()
-            k_copies[b].start()
-        out_copies = []
-
-        def send_out(view, tile_at, n_tiles, slot):
-            for i, (dst, flip) in enumerate(((send_hbm, 1), (keep_hbm, 0))):
-                copy = pltpu.make_async_copy(
-                    view(jnp.bitwise_xor(core, flip)), dst.at[:, pl.ds(tile_at, n_tiles)], out_sem.at[i, slot])
+            for copy in k_copies[b]:
                 copy.start()
-                out_copies.append(copy)
-
-        pos = start + lax.broadcasted_iota(jnp.int32, (1, span), 1)
         for b in range(rows):
             q_copies[b].wait()
-            k_copies[b].wait()
-            tops = []
-            for j in range(draft):
-                s = lax.dot_general(q_v[b, j], k_v[b], (((0,), (0,)), ((), ())),
-                                    preferred_element_type=jnp.float32) * score_scale
-                s = jnp.where(pos < len_ref[b] - draft + 1 + j, s, floor_value)
-                s_v[b, j * heads:(j + 1) * heads, :] = s
-                running = s[:, :LANES]
-                for c in range(1, span // LANES):
-                    running = jnp.maximum(running, s[:, c * LANES:(c + 1) * LANES])
-                tops.append(running)
+            tops = [None] * draft
+            for copy, (lo, hi) in zip(k_copies[b], pieces(b)):
+                copy.wait()
+                pos = start + lo + lax.broadcasted_iota(jnp.int32, (1, hi - lo), 1)
+                for j in range(draft):
+                    s = lax.dot_general(q_v[b, j], k_v[b, :, lo:hi], (((0,), (0,)), ((), ())),
+                                        preferred_element_type=jnp.float32) * score_scale
+                    s = jnp.where(pos < len_ref[b] - draft + 1 + j, s, floor_value)
+                    s_v[b, j * heads:(j + 1) * heads, lo:hi] = s
+                    for c in range((hi - lo) // LANES):
+                        piece = s[:, c * LANES:(c + 1) * LANES]
+                        tops[j] = piece if tops[j] is None else jnp.maximum(tops[j], piece)
             top = jnp.max(jnp.concatenate(tops, axis=0), axis=-1, keepdims=True)
             top_v[b] = jnp.broadcast_to(top, (qrows, LANES))
             w = jnp.exp2(s_v[b] - jnp.maximum(top, floor_guard)).astype(jnp.bfloat16)
@@ -78,13 +77,16 @@
             acc = lax.dot_general(w, k_v[b, :latent, :], (((1,), (1,)), ((), ())),
                                   preferred_element_type=jnp.float32)
             tot_v[b] = jnp.broadcast_to(jnp.sum(total, axis=-1, keepdims=True), (qrows, LANES))
-            for j in range(draft):
-                block = acc[j * heads:(j + 1) * heads].reshape(pairs, 2, owned, latent)
-                for c in range(lat_tiles):
-                    acc_v[b, j, :, :, c] = block[:, :, :, c * LANES:(c + 1) * LANES]
-            for j in range(draft):
-                r = b * draft + j
-                send_out(lambda bit: acc_v.at[b, j, :, bit], r * lat_tiles, lat_tiles, r)
+            acc_v[...] = acc
+            for bit in range(2):
+                @pl.when(core == bit)
+                def _():
+                    for j in range(draft):
+                        for g in range(groups):
+                            dst = keep_ref if g % 2 == bit else send_ref
+                            at = j * heads + g * owned
+                            for c in range(lat_tiles):
+                                dst[g // 2, (b * draft + j) * lat_tiles + c] = acc_v[at:at + owned, c * LANES:(c + 1) * LANES]
         lane = lax.broadcasted_iota(jnp.int32, (owned, LANES), 1)
         for g in range(groups):
             stat = jnp.zeros((owned, LANES), jnp.float32)
@@ -93,10 +95,13 @@
                 at = slice(j * heads + g * owned, j * heads + (g + 1) * owned)
                 stat = jnp.where(lane == r, top_v[b, at, :], stat)
                 stat = jnp.where(lane == count + r, tot_v[b, at, :], stat)
-            stat_v[g // 2, g % 2, 0] = stat
-        send_out(lambda bit: stat_v.at[:, bit], tiles - 1, 1, count)
-        for copy in out_copies:
-            copy.wait()
+            stat_v[g] = stat
+        for bit in range(2):
+            @pl.when(core == bit)
+            def _():
+                for g in range(groups):
+                    dst = keep_ref if g % 2 == bit else send_ref
+                    dst[g // 2, tiles - 1] = stat_v[g]
 
     message = jax.ShapeDtypeStruct((pairs, tiles, owned, LANES), jnp.float32)
     any_space = pl.BlockSpec(memory_space=pl.ANY)
@@ -104,20 +109,19 @@
         kernel,
         out_shape=(message, message),
         in_specs=[any_space, any_space, pl.BlockSpec(memory_space=pltpu.SMEM)],
-        out_specs=(any_space, any_space),
+        out_specs=(pl.BlockSpec(memory_space=pltpu.VMEM),) * 2,
         scratch_shapes=[
             pltpu.VMEM((rows, draft, key_dim, heads), jnp.bfloat16),
             pltpu.VMEM((rows, key_dim, span), jnp.bfloat16),
             pltpu.VMEM((rows, qrows, span), jnp.float32),
-            pltpu.VMEM((rows, draft, pairs, 2, lat_tiles, owned, LANES), jnp.float32),
+            pltpu.VMEM((qrows, latent), jnp.float32),
             pltpu.VMEM((rows, qrows, LANES), jnp.float32),
             pltpu.VMEM((rows, qrows, LANES), jnp.float32),
-            pltpu.VMEM((pairs, 2, 1, owned, LANES), jnp.float32),
+            pltpu.VMEM((groups, owned, LANES), jnp.float32),
             pltpu.SemaphoreType.DMA((rows,)),
-            pltpu.SemaphoreType.DMA((rows,)),
-            pltpu.SemaphoreType.DMA((2, count + 1)),
+            pltpu.SemaphoreType.DMA((rows, FIRST_PARTS)),
         ],
-        compiler_params=pltpu.CompilerParams(vmem_limit_bytes=63 << 20),
+        compiler_params=pltpu.CompilerParams(vmem_limit_bytes=51 << 20),
         name="attend",
     )(queries, cache, lengths)
 

time: 87 us -> 84.8 us (0.975)
  Pallas kernels: 12.1 us -> 10.7 us
    pallas_call x1, Pallas kernels: 10.4 us -> 9.02 us  [attend(): pl.pallas_call(kernel, out_shape=(message, message), in_specs=[any_space,...]
where the time goes in v2:
time: 84.8 us; the launch traced here: 84.5 us
  blocking collectives  61.4 us (72%)
  Pallas kernels  10.7 us (13%)
  starting transfers between devices  8.76 us (10%)
  waiting for transfers between devices  2.31 us (3%)
  local copies, waits for them, and re-layouts  1.28 us (2%)
    all_to_all x1, blocking collectives, body(): lax.all_to_all(values, 'wide', 0, 0, axis_index_groups=along_z, tiled=True)  19.5 us
    all_to_all x1, blocking collectives, body(): lax.all_to_all(mine, 'grp', 0, 0, axis_index_groups=same_core, tiled=True)  18.4 us
    all_to_all x1, blocking collectives, body(): mixed = lax.all_to_all(mixed, 'grp', 0, 0, tiled=True)  13.5 us
    all_to_all x1, blocking collectives, body(): lax.all_to_all(values, 'wide', 0, 0, axis_index_groups=along_y, tiled=True)  9.92 us
    pallas_call x1, Pallas kernels, attend(): pl.pallas_call(kernel, out_shape=(message, message), in_specs=[any_space,...  9.02 us
    ppermute x1, starting transfers between devices, body(): other = lax.ppermute(send, 'grp', [(i, i ^ 1) for i in range(groups)])  8.76 us
    ppermute x1, waiting for transfers between devices, body(): other = lax.ppermute(send, 'grp', [(i, i ^ 1) for i in range(groups)])  2.31 us
  transfers between devices with their start and end apart: 1, of which 1 were waited for; matrix products, arithmetic and copies ran while one was open for 0% of the time, Pallas kernels for 0%

profile of v2, /device:TPU:1, one launch (start us, length us, event | category | flops | bytes accessed | tf_op | source)
XLA Modules:
  0.0 84.5 jit_solution(15101823241533326880)
XLA Ops:
  0.0 0.0 copy-start.2
  0.0 0.7 copy-done.2
  0.7 9.0 %attend.1 = (f32[8,33,8,128]{3,2,1,0:T(8,128)S(1)}, f32[8,33,8,128]{3,2,1,0:T(8,128)S(1)}) custom-call(bf16[2,4,576,128]{3,2,1,0:T(8,128)(2,1)} %bitcast.5, bf16[2,576,2048]{2,1,0:T(8,128)(2,1)} %bitcast.4, s32[2]{0:T(128)S(1)} %copy-done.2), custom_call_target="tpu_custom_call" | custom-call | tf_op jit(solution)/shard_map/attend/pallas_call | solution.py:108
  9.7 8.8 %collective-permute-start = (f32[8,33,8,128]{3,2,1,0:T(8,128)S(1)}, f32[8,33,8,128]{3,2,1,0:T(8,128)S(1)}, u32[]{:S(2)}, u32[]{:S(2)}) collective-permute-start(f32[8,33,8,128]{3,2,1,0:T(8,128)S(1)} %get-tuple-element.8), channel_id=1, source_target_pairs={{0,32},{32,0},{64,96},{96,64},{128,160},{160,128},{192,224},{224,1... | collective-permute-start | bytes 3244040 | tf_op jit(solution)/shard_map/ppermute | solution.py:265
  18.4 2.3 %collective-permute-done.b_ref = f32[8,33,8,128]{3,2,1,0:T(8,128)S(1)} collective-permute-done((f32[8,33,8,128]{3,2,1,0:T(8,128)S(1)}, f32[8,33,8,128]{3,2,1,0:T(8,128)S(1)}, u32[]{:S(2)}, u32[]{:S(2)}) %collective-permute-start) | collective-permute-done | bytes 1081376 | tf_op jit(solution)/shard_map/ppermute | solution.py:265
  20.8 0.6 add_cores.1
  21.4 0.0 copy-start
  21.4 18.4 %all_to_all.20.p_ref = f32[8,33,8,128]{3,2,1,0:T(8,128)S(1)} all-to-all(f32[8,33,8,128]{3,2,1,0:T(8,128)S(1)} %add_cores.1), channel_id=1, replica_groups={{0,64,128,192,256,320,384,448},{32,96,160,224,288,352,416,480},{1,65,12..., dimensions={0} | all-to-all | bytes 2162688 | tf_op jit(solution)/shard_map/all_to_all | solution.py:267
  39.8 0.0 copy-done
  39.8 0.6 up_project.1
  40.4 0.0 copy-start.1
  40.4 9.9 %all_to_all.21.p_ref = f32[4,9,8,128]{3,2,1,0:T(8,128)S(1)} all-to-all(f32[4,9,8,128]{3,2,1,0:T(8,128)S(1)} %up_project.1), channel_id=1, replica_groups={{0,1,2,3},{4,5,6,7},{8,9,10,11},{12,13,14,15},{16,17,18,19},{20,21,22,2..., dimensions={0} | all-to-all | bytes 294912 | tf_op jit(solution)/shard_map/all_to_all | solution.py:269
  50.3 0.1 add_wide.1
  50.5 19.5 %all_to_all.22.p_ref = f32[8,9,8,128]{3,2,1,0:T(8,128)S(1)} all-to-all(f32[8,9,8,128]{3,2,1,0:T(8,128)S(1)} %add_wide.1), channel_id=1, replica_groups={{0,4,8,12,16,20,24,28},{1,5,9,13,17,21,25,29},{2,6,10,14,18,22,26,30},{..., dimensions={0} | all-to-all | bytes 589824 | tf_op jit(solution)/shard_map/all_to_all | solution.py:271
  70.0 0.0 copy-done.1
  70.0 0.4 out_project.1
  70.4 13.5 %all_to_all.23 = f32[16,8,224]{2,1,0:T(8,128)S(1)} all-to-all(f32[16,8,224]{2,1,0:T(8,128)S(1)} %out_project.1), channel_id=1, replica_groups=mesh['grp'=16,'wide'=32] {'grp'}, dimensions={0} | all-to-all | bytes 229376 | tf_op jit(solution)/shard_map/all_to_all | solution.py:273
  83.9 0.6 reshape.3
  (1 shorter events, 0.0 us)
Async XLA Ops:
  0.0 0.7 copy-start.2
  9.7 11.1 %collective-permute-start = (f32[8,33,8,128]{3,2,1,0:T(8,128)S(1)}, f32[8,33,8,128]{3,2,1,0:T(8,128)S(1)}, u32[]{:S(2)}, u32[]{:S(2)}) collective-permute-start(f32[8,33,8,128]{3,2,1,0:T(8,128)S(1)} %get-tuple-element.8), channel_id=1, source_target_pairs={{0,32},{32,0},{64,96},{96,64},{128,160},{160,128},{192,224},{224,1... | collective-permute-start | bytes 3244040 | tf_op jit(solution)/shard_map/ppermute | solution.py:265
  21.4 18.5 %copy-start = (bf16[8,512,128]{2,1,0:T(8,128)(2,1)S(1)}, bf16[8,512,128]{2,1,0:T(8,128)(2,1)}, u32[]{:S(2)}) copy-start(bf16[8,512,128]{2,1,0:T(8,128)(2,1)} %u_ref.1) | copy-start | bytes 3145732
  40.4 29.6 %copy-start.1 = (bf16[1024,224]{0,1:T(8,128)(2,1)S(1)}, bf16[1024,224]{0,1:T(8,128)(2,1)}, u32[]{:S(2)}) copy-start(bf16[1024,224]{0,1:T(8,128)(2,1)} %param.9) | copy-start | bytes 1376260

commit v3 on v2

--- a/solution.py
+++ b/solution.py
@@ -14,7 +14,7 @@
 
 LANES = 128
 SUB = 8
-FIRST_PARTS = 2
+FIRST_PART = 4
 
 
 def split_dot(x, w, contract=0):
@@ -37,11 +37,10 @@
     qrows = draft * heads
 
     def pieces(b):
-        part = span // FIRST_PARTS if b == 0 else span
-        return [(lo, lo + part) for lo in range(0, span, part)]
+        return [(0, span // FIRST_PART), (span // FIRST_PART, span)] if b == 0 else [(0, span)]
 
     def kernel(q_hbm, cache_hbm, len_ref, keep_ref, send_ref,
-               q_v, k_v, s_v, acc_v, top_v, tot_v, stat_v, q_sem, k_sem):
+               q_v, k_v, s_v, acc_v, stat_v, q_sem, k_sem):
         grp = lax.axis_index("grp")
         core = lax.rem(grp, 2)
         start = (grp * lax.axis_size("wide") + lax.axis_index("wide")) * span
@@ -53,6 +52,8 @@
             q_copies[b].start()
             for copy in k_copies[b]:
                 copy.start()
+        lane = lax.broadcasted_iota(jnp.int32, (heads, LANES), 1)
+        stat = jnp.zeros((heads, LANES), jnp.float32)
         for b in range(rows):
             q_copies[b].wait()
             tops = [None] * draft
@@ -68,7 +69,6 @@
                         piece = s[:, c * LANES:(c + 1) * LANES]
                         tops[j] = piece if tops[j] is None else jnp.maximum(tops[j], piece)
             top = jnp.max(jnp.concatenate(tops, axis=0), axis=-1, keepdims=True)
-            top_v[b] = jnp.broadcast_to(top, (qrows, LANES))
             w = jnp.exp2(s_v[b] - jnp.maximum(top, floor_guard)).astype(jnp.bfloat16)
             wide_w = w.astype(jnp.float32)
             total = wide_w[:, :LANES]
@@ -76,7 +76,12 @@
                 total = total + wide_w[:, c * LANES:(c + 1) * LANES]
             acc = lax.dot_general(w, k_v[b, :latent, :], (((1,), (1,)), ((), ())),
                                   preferred_element_type=jnp.float32)
-            tot_v[b] = jnp.broadcast_to(jnp.sum(total, axis=-1, keepdims=True), (qrows, LANES))
+            total = jnp.sum(total, axis=-1, keepdims=True)
+            for j in range(draft):
+                r = b * draft + j
+                at = slice(j * heads, (j + 1) * heads)
+                stat = jnp.where(lane == r, top[at], stat)
+                stat = jnp.where(lane == count + r, total[at], stat)
             acc_v[...] = acc
             for bit in range(2):
                 @pl.when(core == bit)
@@ -87,21 +92,13 @@
                             at = j * heads + g * owned
                             for c in range(lat_tiles):
                                 dst[g // 2, (b * draft + j) * lat_tiles + c] = acc_v[at:at + owned, c * LANES:(c + 1) * LANES]
-        lane = lax.broadcasted_iota(jnp.int32, (owned, LANES), 1)
-        for g in range(groups):
-            stat = jnp.zeros((owned, LANES), jnp.float32)
-            for r in range(count):
-                b, j = r // draft, r % draft
-                at = slice(j * heads + g * owned, j * heads + (g + 1) * owned)
-                stat = jnp.where(lane == r, top_v[b, at, :], stat)
-                stat = jnp.where(lane == count + r, tot_v[b, at, :], stat)
-            stat_v[g] = stat
+        stat_v[...] = stat
         for bit in range(2):
             @pl.when(core == bit)
             def _():
                 for g in range(groups):
                     dst = keep_ref if g % 2 == bit else send_ref
-                    dst[g // 2, tiles - 1] = stat_v[g]
+                    dst[g // 2, tiles - 1] = stat_v[g * owned:(g + 1) * owned, :]
 
     message = jax.ShapeDtypeStruct((pairs, tiles, owned, LANES), jnp.float32)
     any_space = pl.BlockSpec(memory_space=pl.ANY)
@@ -115,11 +112,9 @@
             pltpu.VMEM((rows, key_dim, span), jnp.bfloat16),
             pltpu.VMEM((rows, qrows, span), jnp.float32),
             pltpu.VMEM((qrows, latent), jnp.float32),
-            pltpu.VMEM((rows, qrows, LANES), jnp.float32),
-            pltpu.VMEM((rows, qrows, LANES), jnp.float32),
-            pltpu.VMEM((groups, owned, LANES), jnp.float32),
+            pltpu.VMEM((heads, LANES), jnp.float32),
             pltpu.SemaphoreType.DMA((rows,)),
-            pltpu.SemaphoreType.DMA((rows, FIRST_PARTS)),
+            pltpu.SemaphoreType.DMA((rows, 2)),
         ],
         compiler_params=pltpu.CompilerParams(vmem_limit_bytes=51 << 20),
         name="attend",
@@ -155,14 +150,9 @@
                     t = r * per + c
                     o_ref[a, t] = a_ref[a, t] * ea + b_ref[a, t] * eb
 
-    steps = 4
-    spec = pl.BlockSpec((pairs // steps,) + keep.shape[1:], lambda i: (i, 0, 0, 0))
-    return pl.pallas_call(
-        kernel,
-        grid=(steps,),
+    return pl.pallas_call(
+        kernel,
         out_shape=jax.ShapeDtypeStruct(keep.shape, jnp.float32),
-        in_specs=[spec, spec],
-        out_specs=spec,
         compiler_params=pltpu.CompilerParams(vmem_limit_bytes=32 << 20),
         name="add_cores",
     )(keep, other)

time: 84.8 us -> 84.3 us (level)
  no operation moved by 1% of the time
where the time goes in v3:
time: 84.3 us; the launch traced here: 84 us
  blocking collectives  61.4 us (73%)
  Pallas kernels  10.2 us (12%)
  starting transfers between devices  8.78 us (10%)
  waiting for transfers between devices  2.31 us (3%)
  local copies, waits for them, and re-layouts  1.28 us (2%)
    all_to_all x1, blocking collectives, body(): lax.all_to_all(values, 'wide', 0, 0, axis_index_groups=along_z, tiled=True)  19.5 us
    all_to_all x1, blocking collectives, body(): lax.all_to_all(mine, 'grp', 0, 0, axis_index_groups=same_core, tiled=True)  18.4 us
    all_to_all x1, blocking collectives, body(): mixed = lax.all_to_all(mixed, 'grp', 0, 0, tiled=True)  13.5 us
    all_to_all x1, blocking collectives, body(): lax.all_to_all(values, 'wide', 0, 0, axis_index_groups=along_y, tiled=True)  9.94 us
    ppermute x1, starting transfers between devices, body(): other = lax.ppermute(send, 'grp', [(i, i ^ 1) for i in range(groups)])  8.78 us
    pallas_call x1, Pallas kernels, attend(): pl.pallas_call(kernel, out_shape=(message, message), in_specs=[any_space,...  8.7 us
    ppermute x1, waiting for transfers between devices, body(): other = lax.ppermute(send, 'grp', [(i, i ^ 1) for i in range(groups)])  2.31 us
  transfers between devices with their start and end apart: 1, of which 1 were waited for; matrix products, arithmetic and copies ran while one was open for 0% of the time, Pallas kernels for 0%

profile of v3, /device:TPU:1, one launch (start us, length us, event | category | flops | bytes accessed | tf_op | source)
XLA Modules:
  0.0 84.0 jit_solution(10311362079989640965)
XLA Ops:
  0.0 0.0 copy-start.2
  0.0 0.7 copy-done.2
  0.7 8.7 %attend.1 = (f32[8,33,8,128]{3,2,1,0:T(8,128)S(1)}, f32[8,33,8,128]{3,2,1,0:T(8,128)S(1)}) custom-call(bf16[2,4,576,128]{3,2,1,0:T(8,128)(2,1)} %bitcast.5, bf16[2,576,2048]{2,1,0:T(8,128)(2,1)} %bitcast.4, s32[2]{0:T(128)S(1)} %copy-done.2), custom_call_target="tpu_custom_call" | custom-call | tf_op jit(solution)/shard_map/attend/pallas_call | solution.py:105
  9.4 8.8 %collective-permute-start = (f32[8,33,8,128]{3,2,1,0:T(8,128)S(1)}, f32[8,33,8,128]{3,2,1,0:T(8,128)S(1)}, u32[]{:S(2)}, u32[]{:S(2)}) collective-permute-start(f32[8,33,8,128]{3,2,1,0:T(8,128)S(1)} %get-tuple-element.8), channel_id=1, source_target_pairs={{0,32},{32,0},{64,96},{96,64},{128,160},{160,128},{192,224},{224,1... | collective-permute-start | bytes 3244040 | tf_op jit(solution)/shard_map/ppermute | solution.py:255
  18.1 2.3 %collective-permute-done.b_ref = f32[8,33,8,128]{3,2,1,0:T(8,128)S(1)} collective-permute-done((f32[8,33,8,128]{3,2,1,0:T(8,128)S(1)}, f32[8,33,8,128]{3,2,1,0:T(8,128)S(1)}, u32[]{:S(2)}, u32[]{:S(2)}) %collective-permute-start) | collective-permute-done | bytes 1081376 | tf_op jit(solution)/shard_map/ppermute | solution.py:255
  20.5 0.4 add_cores.1
  20.9 0.0 copy-start
  20.9 18.4 %all_to_all.20.p_ref = f32[8,33,8,128]{3,2,1,0:T(8,128)S(1)} all-to-all(f32[8,33,8,128]{3,2,1,0:T(8,128)S(1)} %add_cores.1), channel_id=1, replica_groups={{0,64,128,192,256,320,384,448},{32,96,160,224,288,352,416,480},{1,65,12..., dimensions={0} | all-to-all | bytes 2162688 | tf_op jit(solution)/shard_map/all_to_all | solution.py:257
  39.3 0.0 copy-done
  39.3 0.6 up_project.1
  39.9 0.0 copy-start.1
  39.9 9.9 %all_to_all.21.p_ref = f32[4,9,8,128]{3,2,1,0:T(8,128)S(1)} all-to-all(f32[4,9,8,128]{3,2,1,0:T(8,128)S(1)} %up_project.1), channel_id=1, replica_groups={{0,1,2,3},{4,5,6,7},{8,9,10,11},{12,13,14,15},{16,17,18,19},{20,21,22,2..., dimensions={0} | all-to-all | bytes 294912 | tf_op jit(solution)/shard_map/all_to_all | solution.py:259
  49.8 0.1 add_wide.1
  50.0 19.5 %all_to_all.22.p_ref = f32[8,9,8,128]{3,2,1,0:T(8,128)S(1)} all-to-all(f32[8,9,8,128]{3,2,1,0:T(8,128)S(1)} %add_wide.1), channel_id=1, replica_groups={{0,4,8,12,16,20,24,28},{1,5,9,13,17,21,25,29},{2,6,10,14,18,22,26,30},{..., dimensions={0} | all-to-all | bytes 589824 | tf_op jit(solution)/shard_map/all_to_all | solution.py:261
  69.5 0.0 copy-done.1
  69.5 0.4 out_project.1
  69.9 13.5 %all_to_all.23 = f32[16,8,224]{2,1,0:T(8,128)S(1)} all-to-all(f32[16,8,224]{2,1,0:T(8,128)S(1)} %out_project.1), channel_id=1, replica_groups=mesh['grp'=16,'wide'=32] {'grp'}, dimensions={0} | all-to-all | bytes 229376 | tf_op jit(solution)/shard_map/all_to_all | solution.py:263
  83.4 0.6 reshape.3
  (1 shorter events, 0.0 us)
Async XLA Ops:
  0.0 0.7 copy-start.2
  9.4 11.1 %collective-permute-start = (f32[8,33,8,128]{3,2,1,0:T(8,128)S(1)}, f32[8,33,8,128]{3,2,1,0:T(8,128)S(1)}, u32[]{:S(2)}, u32[]{:S(2)}) collective-permute-start(f32[8,33,8,128]{3,2,1,0:T(8,128)S(1)} %get-tuple-element.8), channel_id=1, source_target_pairs={{0,32},{32,0},{64,96},{96,64},{128,160},{160,128},{192,224},{224,1... | collective-permute-start | bytes 3244040 | tf_op jit(solution)/shard_map/ppermute | solution.py:255
  20.9 18.5 %copy-start = (bf16[8,512,128]{2,1,0:T(8,128)(2,1)S(1)}, bf16[8,512,128]{2,1,0:T(8,128)(2,1)}, u32[]{:S(2)}) copy-start(bf16[8,512,128]{2,1,0:T(8,128)(2,1)} %u_ref.1) | copy-start | bytes 3145732
  39.9 29.6 %copy-start.1 = (bf16[1024,224]{0,1:T(8,128)(2,1)S(1)}, bf16[1024,224]{0,1:T(8,128)(2,1)}, u32[]{:S(2)}) copy-start(bf16[1024,224]{0,1:T(8,128)(2,1)} %param.9) | copy-start | bytes 1376260

commit v4 on v3

--- a/solution.py
+++ b/solution.py
@@ -55,10 +55,12 @@
         lane = lax.broadcasted_iota(jnp.int32, (heads, LANES), 1)
         stat = jnp.zeros((heads, LANES), jnp.float32)
         for b in range(rows):
-            q_copies[b].wait()
+            if b == 0:
+                q_copies[b].wait()
             tops = [None] * draft
             for copy, (lo, hi) in zip(k_copies[b], pieces(b)):
-                copy.wait()
+                if b == 0:
+                    copy.wait()
                 pos = start + lo + lax.broadcasted_iota(jnp.int32, (1, hi - lo), 1)
                 for j in range(draft):
                     s = lax.dot_general(q_v[b, j], k_v[b, :, lo:hi], (((0,), (0,)), ((), ())),
@@ -68,6 +70,10 @@
                     for c in range((hi - lo) // LANES):
                         piece = s[:, c * LANES:(c + 1) * LANES]
                         tops[j] = piece if tops[j] is None else jnp.maximum(tops[j], piece)
+            if b == 0:
+                for later in range(1, rows):
+                    for copy in [q_copies[later]] + k_copies[later]:
+                        copy.wait()
             top = jnp.max(jnp.concatenate(tops, axis=0), axis=-1, keepdims=True)
             w = jnp.exp2(s_v[b] - jnp.maximum(top, floor_guard)).astype(jnp.bfloat16)
             wide_w = w.astype(jnp.float32)
@@ -82,16 +88,7 @@
                 at = slice(j * heads, (j + 1) * heads)
                 stat = jnp.where(lane == r, top[at], stat)
                 stat = jnp.where(lane == count + r, total[at], stat)
-            acc_v[...] = acc
-            for bit in range(2):
-                @pl.when(core == bit)
-                def _():
-                    for j in range(draft):
-                        for g in range(groups):
-                            dst = keep_ref if g % 2 == bit else send_ref
-                            at = j * heads + g * owned
-                            for c in range(lat_tiles):
-                                dst[g // 2, (b * draft + j) * lat_tiles + c] = acc_v[at:at + owned, c * LANES:(c + 1) * LANES]
+            acc_v[b] = acc
         stat_v[...] = stat
         for bit in range(2):
             @pl.when(core == bit)
@@ -99,6 +96,10 @@
                 for g in range(groups):
                     dst = keep_ref if g % 2 == bit else send_ref
                     dst[g // 2, tiles - 1] = stat_v[g * owned:(g + 1) * owned, :]
+                    for r in range(count):
+                        at = (r % draft) * heads + g * owned
+                        for c in range(lat_tiles):
+                            dst[g // 2, r * lat_tiles + c] = acc_v[r // draft, at:at + owned, c * LANES:(c + 1) * LANES]
 
     message = jax.ShapeDtypeStruct((pairs, tiles, owned, LANES), jnp.float32)
     any_space = pl.BlockSpec(memory_space=pl.ANY)
@@ -111,7 +112,7 @@
             pltpu.VMEM((rows, draft, key_dim, heads), jnp.bfloat16),
             pltpu.VMEM((rows, key_dim, span), jnp.bfloat16),
             pltpu.VMEM((rows, qrows, span), jnp.float32),
-            pltpu.VMEM((qrows, latent), jnp.float32),
+            pltpu.VMEM((rows, qrows, latent), jnp.float32),
             pltpu.VMEM((heads, LANES), jnp.float32),
             pltpu.SemaphoreType.DMA((rows,)),
             pltpu.SemaphoreType.DMA((rows, 2)),

time: 84.3 us -> 84.3 us (level)
  no operation moved by 1% of the time
where the time goes in v4:
time: 84.3 us; the launch traced here: 84 us
  blocking collectives  61.4 us (73%)
  Pallas kernels  10.2 us (12%)
  starting transfers between devices  8.77 us (10%)
  waiting for transfers between devices  2.31 us (3%)
  local copies, waits for them, and re-layouts  1.28 us (2%)
    all_to_all x1, blocking collectives, body(): lax.all_to_all(values, 'wide', 0, 0, axis_index_groups=along_z, tiled=True)  19.5 us
    all_to_all x1, blocking collectives, body(): lax.all_to_all(mine, 'grp', 0, 0, axis_index_groups=same_core, tiled=True)  18.4 us
    all_to_all x1, blocking collectives, body(): mixed = lax.all_to_all(mixed, 'grp', 0, 0, tiled=True)  13.5 us
    all_to_all x1, blocking collectives, body(): lax.all_to_all(values, 'wide', 0, 0, axis_index_groups=along_y, tiled=True)  9.91 us
    ppermute x1, starting transfers between devices, body(): other = lax.ppermute(send, 'grp', [(i, i ^ 1) for i in range(groups)])  8.77 us
    pallas_call x1, Pallas kernels, attend(): pl.pallas_call(kernel, out_shape=(message, message), in_specs=[any_space,...  8.66 us
    ppermute x1, waiting for transfers between devices, body(): other = lax.ppermute(send, 'grp', [(i, i ^ 1) for i in range(groups)])  2.31 us
  transfers between devices with their start and end apart: 1, of which 1 were waited for; matrix products, arithmetic and copies ran while one was open for 0% of the time, Pallas kernels for 0%

profile of v4, /device:TPU:1, one launch (start us, length us, event | category | flops | bytes accessed | tf_op | source)
XLA Modules:
  0.0 84.0 jit_solution(15789196194839372396)
XLA Ops:
  0.0 0.0 copy-start.2
  0.0 0.7 copy-done.2
  0.7 8.7 %attend.1 = (f32[8,33,8,128]{3,2,1,0:T(8,128)S(1)}, f32[8,33,8,128]{3,2,1,0:T(8,128)S(1)}) custom-call(bf16[2,4,576,128]{3,2,1,0:T(8,128)(2,1)} %bitcast.5, bf16[2,576,2048]{2,1,0:T(8,128)(2,1)} %bitcast.4, s32[2]{0:T(128)S(1)} %copy-done.2), custom_call_target="tpu_custom_call" | custom-call | tf_op jit(solution)/shard_map/attend/pallas_call | solution.py:106
  9.3 8.8 %collective-permute-start = (f32[8,33,8,128]{3,2,1,0:T(8,128)S(1)}, f32[8,33,8,128]{3,2,1,0:T(8,128)S(1)}, u32[]{:S(2)}, u32[]{:S(2)}) collective-permute-start(f32[8,33,8,128]{3,2,1,0:T(8,128)S(1)} %get-tuple-element.8), channel_id=1, source_target_pairs={{0,32},{32,0},{64,96},{96,64},{128,160},{160,128},{192,224},{224,1... | collective-permute-start | bytes 3244040 | tf_op jit(solution)/shard_map/ppermute | solution.py:256
  18.1 2.3 %collective-permute-done.b_ref = f32[8,33,8,128]{3,2,1,0:T(8,128)S(1)} collective-permute-done((f32[8,33,8,128]{3,2,1,0:T(8,128)S(1)}, f32[8,33,8,128]{3,2,1,0:T(8,128)S(1)}, u32[]{:S(2)}, u32[]{:S(2)}) %collective-permute-start) | collective-permute-done | bytes 1081376 | tf_op jit(solution)/shard_map/ppermute | solution.py:256
  20.4 0.4 add_cores.1
  20.8 0.0 copy-start
  20.9 18.4 %all_to_all.20.p_ref = f32[8,33,8,128]{3,2,1,0:T(8,128)S(1)} all-to-all(f32[8,33,8,128]{3,2,1,0:T(8,128)S(1)} %add_cores.1), channel_id=1, replica_groups={{0,64,128,192,256,320,384,448},{32,96,160,224,288,352,416,480},{1,65,12..., dimensions={0} | all-to-all | bytes 2162688 | tf_op jit(solution)/shard_map/all_to_all | solution.py:258
  39.3 0.0 copy-done
  39.3 0.6 up_project.1
  39.9 0.0 copy-start.1
  39.9 9.9 %all_to_all.21.p_ref = f32[4,9,8,128]{3,2,1,0:T(8,128)S(1)} all-to-all(f32[4,9,8,128]{3,2,1,0:T(8,128)S(1)} %up_project.1), channel_id=1, replica_groups={{0,1,2,3},{4,5,6,7},{8,9,10,11},{12,13,14,15},{16,17,18,19},{20,21,22,2..., dimensions={0} | all-to-all | bytes 294912 | tf_op jit(solution)/shard_map/all_to_all | solution.py:260
  49.8 0.1 add_wide.1
  49.9 19.5 %all_to_all.22.p_ref = f32[8,9,8,128]{3,2,1,0:T(8,128)S(1)} all-to-all(f32[8,9,8,128]{3,2,1,0:T(8,128)S(1)} %add_wide.1), channel_id=1, replica_groups={{0,4,8,12,16,20,24,28},{1,5,9,13,17,21,25,29},{2,6,10,14,18,22,26,30},{..., dimensions={0} | all-to-all | bytes 589824 | tf_op jit(solution)/shard_map/all_to_all | solution.py:262
  69.5 0.0 copy-done.1
  69.5 0.4 out_project.1
  69.9 13.5 %all_to_all.23 = f32[16,8,224]{2,1,0:T(8,128)S(1)} all-to-all(f32[16,8,224]{2,1,0:T(8,128)S(1)} %out_project.1), channel_id=1, replica_groups=mesh['grp'=16,'wide'=32] {'grp'}, dimensions={0} | all-to-all | bytes 229376 | tf_op jit(solution)/shard_map/all_to_all | solution.py:264
  83.4 0.6 reshape.3
  (1 shorter events, 0.0 us)
Async XLA Ops:
  0.0 0.7 copy-start.2
  9.3 11.1 %collective-permute-start = (f32[8,33,8,128]{3,2,1,0:T(8,128)S(1)}, f32[8,33,8,128]{3,2,1,0:T(8,128)S(1)}, u32[]{:S(2)}, u32[]{:S(2)}) collective-permute-start(f32[8,33,8,128]{3,2,1,0:T(8,128)S(1)} %get-tuple-element.8), channel_id=1, source_target_pairs={{0,32},{32,0},{64,96},{96,64},{128,160},{160,128},{192,224},{224,1... | collective-permute-start | bytes 3244040 | tf_op jit(solution)/shard_map/ppermute | solution.py:256
  20.8 18.5 %copy-start = (bf16[8,512,128]{2,1,0:T(8,128)(2,1)S(1)}, bf16[8,512,128]{2,1,0:T(8,128)(2,1)}, u32[]{:S(2)}) copy-start(bf16[8,512,128]{2,1,0:T(8,128)(2,1)} %u_ref.1) | copy-start | bytes 3145732
  39.9 29.6 %copy-start.1 = (bf16[1024,224]{0,1:T(8,128)(2,1)S(1)}, bf16[1024,224]{0,1:T(8,128)(2,1)}, u32[]{:S(2)}) copy-start(bf16[1024,224]{0,1:T(8,128)(2,1)} %param.9) | copy-start | bytes 1376260
